TPU v7x, 32 devices: a whole 2x2x4 slice. The times are simulated.
32 devices in a mesh: dp: 4 (over z), expert: 8 (over y, x, core).
Axes of the slice: x: 2, y: 2, z: 4, core: 2. Of those that a mesh axis runs over, the one named last changes fastest.
Arguments:
- residual_in: bfloat16 [4096, 2048], P(('dp', 'expert')), may hold values from -40 to 40
- attention_gain: float32 [2048], replicated, may hold values from 0.25 to 1.75
- query_weight: bfloat16 [2048, 2048], P(None, 'expert'), may hold values from -0.125 to 0.125
- key_weight: bfloat16 [2048, 2048], P(None, 'expert'), may hold values from -0.125 to 0.125
- value_weight: bfloat16 [2048, 2048], P(None, 'expert'), may hold values from -0.125 to 0.125
- output_weight: bfloat16 [2048, 2048], P('expert'), may hold values from -0.125 to 0.125
- prompt_keys: bfloat16 [12, 2048, 2048], P('dp', None, 'expert'), may hold values from -220 to 220
- prompt_values: bfloat16 [12, 2048, 2048], P('dp', None, 'expert'), may hold values from -12 to 12
- group_index: int32 [4, 32], P('dp'), may hold values from 0 to 2, never falling along the last dimension, each value on 1 to 16 neighbouring positions
- prompt_length: int32 [12], P('dp'), may hold values from 1 to 2048, 12288 in all
- own_length: int32 [128], P('dp'), may hold values from 1 to 32
- expert_gain: float32 [2048], replicated, may hold values from 0.25 to 1.75
- expert_ids: int32 [4096, 8], P(('dp', 'expert')), may hold values from 0 to 31, all different within a row; in each aligned block of 128 rows (0 to 127, 128 to 255, ...) at most 48 rows name the same one
- expert_mix: float32 [4096, 8], P(('dp', 'expert')), may hold values from 0.02 to 0.3
- gate_weight: bfloat16 [32, 2048, 1024], P(('dp', 'expert')), may hold values from -0.125 to 0.125
- up_weight: bfloat16 [32, 2048, 1024], P(('dp', 'expert')), may hold values from -0.125 to 0.125
- down_weight: bfloat16 [32, 1024, 2048], P(('dp', 'expert')), may hold values from -0.1875 to 0.1875
Outputs:
- attention_update: bfloat16 [4096, 2048], P(('dp', 'expert'))
- expert_update: bfloat16 [4096, 2048], P(('dp', 'expert'))
Inputs may be any that keep to these rules, and one draw needn't show every extreme that they name: `group_index`: each row holds the 32 requests of one index of dp; a group's requests are consecutive, every group has 1 to 16 requests and some group exactly 16. `prompt_length`: some prompt is exactly 2048 long. `expert_ids`: a token's 8 experts differ; among the 128 rows of one device no expert is named more than 48 times, a bound that some block reaches.
All inputs are finite; a program needn't handle non-finite values. No bound on the sum of `prompt_length` on one device may be relied on, other than what follows from the above.
Results may differ from a plain program's by a relative error of at most 0.025.
The roundings to bfloat16 on the way count: a program that leaves them out, or rounds other values in their place, can miss the bound.
Values may be sent and summed in bfloat16 or wider, within the bound.
A program may use at most 128 MiB of HBM per device.

v0:
```python
import jax
import jax.numpy as jnp
from jax import lax
from jax.sharding import PartitionSpec as P

HD = 128
FF = 1024
TOP = 8
GSIZE = 16
SB = 32


epsilon = 1e-06


def rms_scale(values, gain):
    widened = values.astype(jnp.float32)
    spread = jnp.mean(widened * widened, axis=-1, keepdims=True)
    return (widened * lax.rsqrt(spread + epsilon) * gain).astype(jnp.bfloat16)


def expert_block(block, gate_weight, up_weight, down_weight):
    shape_kept = block.shape
    flat = block.reshape(-1, shape_kept[-1])
    gated = jnp.dot(flat, gate_weight[0], preferred_element_type=jnp.float32)
    lifted = jnp.dot(flat, up_weight[0], preferred_element_type=jnp.float32)
    hidden = (jax.nn.silu(gated) * lifted).astype(jnp.bfloat16)
    produced = jnp.dot(hidden, down_weight[0], preferred_element_type=jnp.float32).astype(
        jnp.bfloat16
    )
    return produced.reshape(shape_kept)


def per_device(
    residual_in,
    attention_gain,
    query_weight,
    key_weight,
    value_weight,
    output_weight,
    prompt_keys,
    prompt_values,
    group_index,
    prompt_length,
    own_length,
    expert_gain,
    expert_ids,
    expert_mix,
    gate_weight,
    up_weight,
    down_weight,
):
    tok_rows, width = residual_in.shape
    local_width = query_weight.shape[1]
    heads_here = local_width // HD
    requests = group_index.shape[1]
    longest = prompt_keys.shape[1]
    groups_here = prompt_keys.shape[0]
    normed = rms_scale(residual_in, attention_gain)
    piece = lax.all_gather(normed, "expert", axis=0, tiled=True)
    query_part = jnp.dot(piece, query_weight, preferred_element_type=jnp.float32).astype(
        jnp.bfloat16
    )
    key_part = jnp.dot(piece, key_weight, preferred_element_type=jnp.float32).astype(jnp.bfloat16)
    value_part = jnp.dot(piece, value_weight, preferred_element_type=jnp.float32).astype(
        jnp.bfloat16
    )
    projected = jnp.concatenate([query_part, key_part, value_part], axis=1)
    layout = (requests, SB, heads_here, HD)
    queries = projected[:, :local_width].reshape(layout)
    new_keys = projected[:, local_width : 2 * local_width].reshape(layout)
    new_values = projected[:, 2 * local_width :].reshape(layout)
    scale = HD ** (-0.5)
    positions = jnp.arange(SB, dtype=jnp.int32)
    own_scores = (
        jnp.einsum("rihd,rjhd->rhij", queries, new_keys, preferred_element_type=jnp.float32) * scale
    )
    own_scores = jnp.where(
        positions[None, None, None, :] < own_length[:, None, None, None], own_scores, -jnp.inf
    )
    member = group_index[0]
    prompt_positions = jnp.arange(longest, dtype=jnp.int32)

    def group_step(group, attended):
        first = jnp.sum((member < group).astype(jnp.int32))
        start = jnp.minimum(first, requests - GSIZE)
        window_queries = lax.dynamic_slice_in_dim(queries, start, GSIZE, 0)
        group_keys = lax.dynamic_index_in_dim(prompt_keys, group, 0, keepdims=False).reshape(
            longest, heads_here, HD
        )
        group_values = lax.dynamic_index_in_dim(prompt_values, group, 0, keepdims=False).reshape(
            longest, heads_here, HD
        )
        scores = (
            jnp.einsum(
                "rihd,jhd->rhij", window_queries, group_keys, preferred_element_type=jnp.float32
            )
            * scale
        )
        limit = lax.dynamic_index_in_dim(prompt_length, group, 0, keepdims=False)
        scores = jnp.where(prompt_positions < limit, scores, -jnp.inf)
        window_own = lax.dynamic_slice_in_dim(own_scores, start, GSIZE, 0)
        highest = jnp.maximum(jnp.max(scores, axis=-1), jnp.max(window_own, axis=-1))
        prompt_weights = jnp.exp(scores - highest[..., None]).astype(jnp.bfloat16)
        own_weights = jnp.exp(window_own - highest[..., None]).astype(jnp.bfloat16)
        window_values = lax.dynamic_slice_in_dim(new_values, start, GSIZE, 0)
        summed = jnp.einsum(
            "rhij,jhd->rihd", prompt_weights, group_values, preferred_element_type=jnp.float32
        )
        summed = summed + jnp.einsum(
            "rhij,rjhd->rihd", own_weights, window_values, preferred_element_type=jnp.float32
        )
        totals = jnp.sum(prompt_weights, axis=-1, dtype=jnp.float32) + jnp.sum(
            own_weights, axis=-1, dtype=jnp.float32
        )
        result = (summed / jnp.transpose(totals, (0, 2, 1))[..., None]).astype(jnp.bfloat16)
        inside = lax.dynamic_slice_in_dim(member, start, GSIZE, 0) == group
        current = lax.dynamic_slice_in_dim(attended, start, GSIZE, 0)
        merged = jnp.where(inside[:, None, None, None], result, current)
        return lax.dynamic_update_slice_in_dim(attended, merged, start, 0)

    attended = lax.fori_loop(0, groups_here, group_step, jnp.zeros(layout, jnp.bfloat16))
    flat_attended = attended.reshape(requests * SB, local_width)
    piece = flat_attended
    attention_update = lax.psum_scatter(
        jnp.dot(piece, output_weight, preferred_element_type=jnp.float32).astype(jnp.bfloat16),
        "expert",
        scatter_dimension=0,
        tiled=True,
    )
    expert_input = rms_scale(
        residual_in.astype(jnp.float32) + attention_update.astype(jnp.float32), expert_gain
    )
    data_groups = lax.axis_size("dp")
    expert_groups = lax.axis_size("expert")
    devices = data_groups * expert_groups
    hidden_split = FF // gate_weight.shape[2]
    experts = devices // hidden_split
    capacity = max(2, tok_rows * TOP * 3 // (2 * experts))
    chosen = expert_ids.reshape(-1)
    routes_here = chosen.shape[0]
    owners = jnp.arange(routes_here, dtype=jnp.int32) // TOP
    matches = (chosen[:, None] == jnp.arange(experts, dtype=jnp.int32)[None, :]).astype(jnp.int32)
    slots = jnp.sum((jnp.cumsum(matches, axis=0) - matches) * matches, axis=1)
    table = (
        jnp.full((experts * capacity,), tok_rows, jnp.int32)
        .at[chosen * capacity + slots]
        .set(owners)
    )
    padded = jnp.concatenate([expert_input, jnp.zeros((1, width), jnp.bfloat16)], axis=0)
    outgoing = jnp.broadcast_to(
        padded[table].reshape(experts, 1, capacity, width), (experts, hidden_split, capacity, width)
    )
    outgoing = outgoing.reshape(devices, capacity, width)
    returned = lax.all_to_all(
        expert_block(
            lax.all_to_all(outgoing, ("dp", "expert"), split_axis=0, concat_axis=0, tiled=True),
            gate_weight,
            up_weight,
            down_weight,
        ),
        ("dp", "expert"),
        split_axis=0,
        concat_axis=0,
        tiled=True,
    )
    pieces = returned.reshape(experts, hidden_split, capacity, width)[chosen, :, slots]
    blended = jnp.sum(pieces.astype(jnp.float32), axis=1) * expert_mix.reshape(-1)[:, None]
    expert_update = jnp.sum(blended.reshape(tok_rows, TOP, width), axis=1).astype(jnp.bfloat16)
    return (attention_update, expert_update)


def solution(mesh):
    in_specs = (
        P(("dp", "expert"), None),
        P(),
        P(None, "expert"),
        P(None, "expert"),
        P(None, "expert"),
        P("expert", None),
        P("dp", None, "expert"),
        P("dp", None, "expert"),
        P("dp", None),
        P("dp"),
        P("dp"),
        P(),
        P(("dp", "expert"), None),
        P(("dp", "expert"), None),
        P(("dp", "expert"), None, None),
        P(("dp", "expert"), None, None),
        P(("dp", "expert"), None, None),
    )
    out_specs = (P(("dp", "expert"), None), P(("dp", "expert"), None))
    return jax.shard_map(
        per_device, mesh=mesh, in_specs=in_specs, out_specs=out_specs, check_vma=False
    )
```

profile of v0, /device:TPU:0, one launch (start us, length us, event | category | flops | bytes accessed | tf_op | source)
XLA Modules:
  0.0 554.8 jit_solution(12098482507784002697)
XLA Ops:
  11.4 38.8 %all-gather.2.cloned.1.call-done = bf16[1024,2048]{1,0:T(8,128)(2,1)} async-done(((bf16[128,2048]{1,0:T(8,128)(2,1)}), bf16[1024,2048]{1,0:T(8,128)(2,1)}) %all-gather.2.cloned.1.call-update) | async-done | bytes 4194320 | tf_op jit(solution)/shard_map/all_gather | solution.py:60
  50.2 3.7 convolution_convert_fusion.4
  54.9 3.4 convolution_convert_fusion.3
  58.5 3.7 convolution_convert_fusion.2
  63.2 2.5 fusion.23
  66.9 63.7 %while.14 = (s32[]{:T(128)}, bf16[32,32,2,128]{3,2,1,0:T(2,128)(2,1)}, s32[32]{0:T(128)S(1)}, bf16[3,2048,256]{2,1,0:T(8,128)(2,1)}, s32[3]{0:T(128)S(1)}, /*ind...) while((s32[]{:T(128)}, ...), condition=%wide.region_7.8_spmd.clone, body=%wide.region_1.7_spmd.clone.sunk | while | flops 1110081664 | bytes 90120776 | solution.py:122
  81.1 5.2 convolution_bitcast_fusion.3
  93.9 2.5 fusion.76
  102.3 5.2 convolution_bitcast_fusion.3
  115.1 2.5 fusion.76
  123.5 5.2 convolution_bitcast_fusion.3
  130.6 4.3 convolution_convert_fusion.1
  135.4 9.0 %reduce-window.6 = s32[32,8,128]{2,1,0:T(8,128)S(1)} reduce-window(s32[32,8,128]{2,1,0:T(8,128)S(1)} %fusion.34, s32[]{:T(128)} %constant.97.clone.1), window={size=1x1x128 pad=0_0x0_0x127_0}, to_apply=%region_10.11 | reduce-window | flops 4161536 | bytes 262148 | tf_op jit(solution)/shard_map/reduce-window
  144.9 4.3 scatter_custom_fusion
  149.3 37.3 %reduce-scatter.2.cloned.1.call-done = bf16[128,2048]{1,0:T(8,128)(2,1)} async-done(((bf16[1024,2048]{1,0:T(8,128)(2,1)}), bf16[128,2048]{1,0:T(8,128)(2,1)}) %reduce-scatter.2.cloned.1.call-update) | async-done | bytes 524304 | tf_op jit(solution)/shard_map/reduce_scatter | solution.py:125
  189.2 7.1 %gather_fusion = bf16[1536,2048]{1,0:T(8,128)(2,1)} fusion(bf16[129,2048]{1,0:T(8,128)(2,1)S(1)} %concatenate.6, s32[2048]{0:T(1024)S(1)} %pad_clamp_fusion), kind=kCustom, calls=%fused_computation | custom fusion | bytes 12589056 | tf_op jit(solution)/shard_map/gather | solution.py:152
  196.3 143.2 %all_to_all.10 = bf16[32,48,2048]{2,1,0:T(8,128)(2,1)S(1)} all-to-all(bf16[32,48,2048]{2,1,0:T(8,128)(2,1)} %bitcast.126), channel_id=1, replica_groups=mesh['dp'=4,'expert'=8] {'dp','expert'}, dimensions={0} | all-to-all | bytes 12582912 | tf_op jit(solution)/shard_map/all_to_all | solution.py:157
  339.5 2.6 copy-done.8
  342.1 8.4 %fusion.20 = f32[1536,1024]{1,0:T(8,128)} fusion(bf16[1536,2048]{1,0:T(8,128)(2,1)S(1)} %bitcast.129, bf16[1,2048,1024]{2,1,0:T(8,128)(2,1)S(1)} %copy-done.13), kind=kOutput, calls=%fused_computation.42 | convolution fusion | flops 6442450944 | bytes 16777216 | tf_op jit(solution)/shard_map/dot_general | solution.py:25
  350.5 20.6 %convolution_convert_fusion = bf16[1536,2048]{1,0:T(8,128)(2,1)} fusion(bf16[1,1024,2048]{2,1,0:T(8,128)(2,1)} %param.35, f32[1536,1024]{1,0:T(8,128)} %fusion.20, bf16[1536,2048]{1,0:T(8,128)(2,1)} %bitcast.130, bf16[1,2048,1024]{2,1,0:T(8,128)(2,1)} %param.34), kind=kOutput, calls=%fused_computation.38 | convolution fusion | flops 12897484800 | bytes 27262976 | tf_op jit(solution)/shard_map/dot_general | solution.py:28
  371.1 4.1 all-to-all-start.1
  375.4 139.7 %all-to-all-done.1 = bf16[32,48,2048]{2,1,0:T(8,128)(2,1)} async-done(((bf16[32,48,2048]{2,1,0:T(8,128)(2,1)}), bf16[32,48,2048]{2,1,0:T(8,128)(2,1)}, u32[]{:S(2)}, u32[]{:S(2)}) %all-to-all-start.1) | async-done | bytes 6291488 | tf_op jit(solution)/shard_map/all_to_all | solution.py:155
  515.1 25.5 %gather_fusion.1 = bf16[1024,2048]{1,0:T(8,128)(2,1)} fusion(bf16[32,48,2048]{2,1,0:T(8,128)(2,1)} %all-to-all-done.1, s32[1024]{0:T(1024)S(1)} %bitcast.123), kind=kCustom, calls=%fused_computation.1 | custom fusion | bytes 8396800 | tf_op jit(solution)/shard_map/gather | solution.py:167
  540.7 7.3 %fusion.15 = bf16[128,2048]{1,0:T(8,128)(2,1)} fusion(bf16[1024,2048]{1,0:T(8,128)(2,1)} %gather_fusion.1, f32[128,8]{1,0:T(8,128)S(1)} %copy.79), kind=kLoop, calls=%fused_computation.37 | loop fusion | flops 6029312 | bytes 4722688 | tf_op jit(solution)/shard_map/reduce_sum | solution.py:169
  (142 shorter events, 51.8 us)
Async XLA Ops:
  7.2 123.5 %copy-start = (bf16[256,2048]{1,0:T(8,128)(2,1)S(1)}, bf16[256,2048]{1,0:T(8,128)(2,1)}, u32[]{:S(2)}) copy-start(bf16[256,2048]{1,0:T(8,128)(2,1)} %param.24) | copy-start | bytes 3145732
  7.2 47.7 %copy-start.14 = (bf16[2048,256]{1,0:T(8,128)(2,1)S(1)}, bf16[2048,256]{1,0:T(8,128)(2,1)}, u32[]{:S(2)}) copy-start(bf16[2048,256]{1,0:T(8,128)(2,1)} %param.22) | copy-start | bytes 3145732
  7.2 43.0 %all-gather.2.cloned.1.call-start = ((), (), s32[]{:S(2)}) async-start(), calls=%async_computation.3 | async-start | bytes 4718592 | tf_op jit(solution)/shard_map/all_gather | solution.py:60
  10.7 175.9 %reduce-scatter.2.cloned.1.call-start = ((), (), s32[]{:S(2)}) async-start(), calls=%async_computation.4 | async-start | bytes 4718592 | tf_op jit(solution)/shard_map/reduce_scatter | solution.py:125
  58.3 8.6 %copy-start.9 = (s32[1,32]{1,0:T(1,128)S(1)}, s32[1,32]{1,0:T(1,128)}, u32[]{:S(2)}) copy-start(s32[1,32]{1,0:T(1,128)} %param.27) | copy-start | bytes 388
  58.4 8.6 %copy-start.15 = (s32[3]{0:T(128)S(1)}, s32[3]{0:T(128)}, u32[]{:S(2)}) copy-start(s32[3]{0:T(128)} %param.28) | copy-start | bytes 40
  75.1 4.8 copy-start.2
  75.2 2.6 copy-start.3
  81.0 5.3 copy-start.4
  81.0 5.3 copy-start.7
  96.4 4.8 copy-start.2
  96.4 2.6 copy-start.3
  102.3 5.3 copy-start.4
  102.3 5.3 copy-start.7
  117.6 4.8 copy-start.2
  123.5 5.3 copy-start.4
  123.5 5.3 copy-start.7
  130.6 4.3 copy-start.11
  130.6 55.9 %copy-start.6 = (bf16[128,2048]{1,0:T(8,128)(2,1)S(1)}, bf16[128,2048]{1,0:T(8,128)(2,1)}, u32[]{:S(2)}) copy-start(bf16[128,2048]{1,0:T(8,128)(2,1)} %param.19) | copy-start | bytes 1572868
  130.6 57.2 %copy-start.10 = (f32[2048]{0:T(1024)S(1)}, f32[2048]{0:T(1024)}, u32[]{:S(2)}) copy-start(f32[2048]{0:T(1024)} %param.30) | copy-start | bytes 24580
  196.3 145.8 %copy-start.13 = (bf16[1,2048,1024]{2,1,0:T(8,128)(2,1)S(1)}, bf16[1,2048,1024]{2,1,0:T(8,128)(2,1)}, u32[]{:S(2)}) copy-start(bf16[1,2048,1024]{2,1,0:T(8,128)(2,1)} %param.33) | copy-start | bytes 12582916
  371.1 4.1 copy-start.12
  371.1 144.0 %all-to-all-start.1 = ((bf16[32,48,2048]{2,1,0:T(8,128)(2,1)}), bf16[32,48,2048]{2,1,0:T(8,128)(2,1)}, u32[]{:S(2)}, u32[]{:S(2)}) async-start(bf16[32,48,2048]{2,1,0:T(8,128)(2,1)} %bitcast.128), calls=%async_computation.2 | async-start | bytes 12582912 | tf_op jit(solution)/shard_map/all_to_all | solution.py:155
  515.1 32.9 %copy-start.1 = (bf16[256,2048]{1,0:T(8,128)(2,1)S(1)}, bf16[256,2048]{1,0:T(8,128)(2,1)}, u32[]{:S(2)}) copy-start(bf16[256,2048]{1,0:T(8,128)(2,1)} %param.24) | copy-start | bytes 3145732
  (5 other events, 7.6 us)
Sparse Core Ops, SparseCore 0:
  10.8 39.4 all-gather.1
  135.1 51.4 reduce-scatter.1
where the time goes:
time: 556 us; the launch traced here: 555 us
  waiting for transfers between devices  216 us (39%)
  blocking collectives  143 us (26%)
  matrix products  70.6 us (13%)
  local copies, waits for them, and re-layouts  64.9 us (12%)
  other arithmetic  39.4 us (7%)
  between operations  14.2 us (3%)
    all_to_all x1, blocking collectives, per_device(): lax.all_to_all(outgoing, ('dp', 'expert'), split_axis=0, concat_axis=0, t...  143 us
    all_to_all x1, waiting for transfers between devices, per_device(): lax.all_to_all(expert_block(lax.all_to_all(outgoing, ('dp', 'expert'), sp...  140 us
    all_gather x1, waiting for transfers between devices, per_device(): piece = lax.all_gather(normed, 'expert', axis=0, tiled=True)  38.8 us
    reduce_scatter x1, waiting for transfers between devices, per_device(): lax.psum_scatter(jnp.dot(piece, output_weight, preferred_element_type=jnp...  37.3 us
    gather x1, local copies, waits for them, and re-layouts, per_device(): returned.reshape(experts, hidden_split, capacity, width)[chosen, :, slots]  25.5 us
    dot_general x1, matrix products, expert_block(): jnp.dot(hidden, down_weight[0], preferred_element_type=jnp.float32)  20.6 us
    dot_general x3, matrix products, group_step(): jnp.einsum('rhij,jhd->rihd', prompt_weights, group_values, preferred_elem...  15.6 us
  transfers between devices with their start and end apart: 3, of which 3 were waited for; matrix products, arithmetic and copies ran while one was open for 3% of the time, Pallas kernels for 0%

commit v1 on v0

--- a/solution.py
+++ b/solution.py
@@ -1,6 +1,9 @@
+import functools
 import jax
 import jax.numpy as jnp
 from jax import lax
+from jax.experimental import pallas as pl
+from jax.experimental.pallas import tpu as pltpu
 from jax.sharding import PartitionSpec as P
 
 HD = 128
@@ -29,6 +32,491 @@
         jnp.bfloat16
     )
     return produced.reshape(shape_kept)
+
+
+MESH = pl.DeviceIdType.MESH
+
+
+def plane_place():
+    line = lax.axis_index("dp")
+    spot = lax.axis_index("expert")
+    core = lax.rem(spot, 2)
+    across = lax.rem(spot // 2, 2)
+    upward = spot // 4
+    return line, spot, core, across, upward
+
+
+def greet(nz, line, spots):
+    barrier = pltpu.get_barrier_semaphore()
+    for other in spots:
+        pl.semaphore_signal(
+            barrier, inc=1, device_id={"dp": line, "expert": other}, device_id_type=MESH
+        )
+    if nz == 1:
+        pl.semaphore_wait(barrier, len(spots))
+        return
+    spot = lax.axis_index("expert")
+
+    @pl.when(line > 0)
+    def _():
+        pl.semaphore_signal(
+            barrier, inc=1, device_id={"dp": line - 1, "expert": spot}, device_id_type=MESH
+        )
+
+    @pl.when(line < nz - 1)
+    def _():
+        pl.semaphore_signal(
+            barrier, inc=1, device_id={"dp": line + 1, "expert": spot}, device_id_type=MESH
+        )
+
+    ends = jnp.where(line > 0, 1, 0) + jnp.where(line < nz - 1, 1, 0)
+    pl.semaphore_wait(barrier, len(spots) + ends)
+
+
+def gather_kernel(nz, x_ref, out_ref, local_sem, send, recv):
+    line, spot, core, across, upward = plane_place()
+    xn = spot + 2 - 4 * across
+    yn = spot + 4 - 8 * upward
+    dn = xn + yn - spot
+    cn = spot + 1 - 2 * core
+    zi = line if nz > 1 else 0
+    rows = x_ref.shape[0]
+    half = rows // 2
+    whole, first, second = pl.ds(0, rows), pl.ds(0, half), pl.ds(half, half)
+
+    def move(kind, zp, block, part, to, source=None):
+        return pltpu.make_async_remote_copy(
+            src_ref=out_ref.at[zp, block, part] if source is None else source,
+            dst_ref=out_ref.at[zp, block, part],
+            send_sem=send.at[kind, zp],
+            recv_sem=recv.at[kind, zp],
+            device_id={"dp": line, "expert": to},
+            device_id_type=MESH,
+        )
+
+    def along(kind, zp, to, source=None):
+        return pltpu.make_async_remote_copy(
+            src_ref=out_ref.at[zp, spot] if source is None else source,
+            dst_ref=out_ref.at[zp, spot],
+            send_sem=send.at[kind, zp],
+            recv_sem=recv.at[0, zp],
+            device_id={"dp": to, "expert": spot},
+            device_id_type=MESH,
+        )
+
+    local = pltpu.make_async_copy(x_ref, out_ref.at[zi, spot], local_sem)
+    local.start()
+    greet(nz, line, (xn, yn, cn))
+
+    steps = [(0, 0)] + [(s, way) for s in range(1, nz) for way in (-1, 1)]
+
+    def place(s, way):
+        zp = zi + way * s
+        valid = None if s == 0 else (zp >= 0 if way < 0 else zp <= nz - 1)
+        return zp, valid
+
+    def guarded(valid, body):
+        if valid is None:
+            body()
+        else:
+            pl.when(valid)(body)
+
+    def begin(s, way):
+        zp, valid = place(s, way)
+
+        def body():
+            source = x_ref if s == 0 else None
+            if s > 0:
+                along(0, zp, line).wait_recv()
+            if nz > 1 and way <= 0:
+
+                @pl.when(line < nz - 1)
+                def _():
+                    along(0, zp, line + 1, source).start()
+
+            if nz > 1 and way >= 0:
+
+                @pl.when(line > 0)
+                def _():
+                    along(10, zp, line - 1, source).start()
+
+            move(1, zp, spot, whole, xn, source).start()
+            move(2, zp, spot, whole, yn, source).start()
+            move(5, zp, spot, whole, cn, source).start()
+
+        guarded(valid, body)
+
+    def middle(s, way):
+        zp, valid = place(s, way)
+
+        def body():
+            move(1, zp, xn, whole, xn).wait_recv()
+            move(3, zp, xn, first, yn).start()
+            move(6, zp, xn, whole, cn).start()
+            move(2, zp, yn, whole, yn).wait_recv()
+            move(4, zp, yn, second, xn).start()
+            move(7, zp, yn, whole, cn).start()
+
+        guarded(valid, body)
+
+    def last(s, way):
+        zp, valid = place(s, way)
+
+        def body():
+            move(3, zp, dn, first, yn).wait_recv()
+            move(8, zp, dn, first, cn).start()
+            move(4, zp, dn, second, xn).wait_recv()
+            move(9, zp, dn, second, cn).start()
+
+        guarded(valid, body)
+
+    for s in range(nz + 2):
+        for entry in steps:
+            if entry[0] == s:
+                begin(*entry)
+        for entry in steps:
+            if entry[0] == s - 1:
+                middle(*entry)
+        for entry in steps:
+            if entry[0] == s - 2:
+                last(*entry)
+
+    def finish(s, way):
+        zp, valid = place(s, way)
+
+        def body():
+            if nz > 1 and way <= 0:
+
+                @pl.when(line < nz - 1)
+                def _():
+                    along(0, zp, line + 1).wait_send()
+
+            if nz > 1 and way >= 0:
+
+                @pl.when(line > 0)
+                def _():
+                    along(10, zp, line - 1).wait_send()
+
+            sibling = cn - spot
+            for kind, block, part, to in (
+                (1, spot, whole, xn),
+                (2, spot, whole, yn),
+                (3, xn, first, yn),
+                (4, yn, second, xn),
+            ):
+                move(kind, zp, block, part, to).wait_send()
+            for kind, block, part in (
+                (5, spot, whole),
+                (6, xn, whole),
+                (7, yn, whole),
+                (8, dn, first),
+                (9, dn, second),
+            ):
+                move(kind, zp, block, part, cn).wait_send()
+                move(kind, zp, block + sibling, part, cn).wait_recv()
+
+        guarded(valid, body)
+
+    for entry in steps:
+        finish(*entry)
+    local.wait()
+
+
+def gather_rows(x, nz, number):
+    rows, width = x.shape
+    return pl.pallas_call(
+        functools.partial(gather_kernel, nz),
+        out_shape=jax.ShapeDtypeStruct((nz, 8, rows, width), x.dtype),
+        in_specs=[pl.BlockSpec(memory_space=pl.ANY)],
+        out_specs=pl.BlockSpec(memory_space=pl.ANY),
+        scratch_shapes=[
+            pltpu.SemaphoreType.DMA,
+            pltpu.SemaphoreType.DMA((11, nz)),
+            pltpu.SemaphoreType.DMA((10, nz)),
+        ],
+        compiler_params=pltpu.CompilerParams(collective_id=number, has_side_effects=True),
+    )(x)
+
+
+def scatter_kernel(
+    nz, p_ref, out_ref, mine, sib, xa, ya, yb, xb, below, above, local, send, recv
+):
+    line, spot, core, across, upward = plane_place()
+    xn = spot + 2 - 4 * across
+    yn = spot + 4 - 8 * upward
+    cn = spot + 1 - 2 * core
+    zi = line if nz > 1 else 0
+    rows = out_ref.shape[0]
+    half = rows // 2
+    first, second = pl.ds(0, half), pl.ds(half, half)
+    here = 2 * upward + across
+    beside = here + 1 - 2 * across
+    over = here + 2 - 4 * upward
+    apart = beside + over - here
+
+    def sibling(zp, q):
+        return pltpu.make_async_remote_copy(
+            src_ref=p_ref.at[zp, 2 * q + 1 - core],
+            dst_ref=sib.at[zp, q],
+            send_sem=send.at[q, zp],
+            recv_sem=recv.at[q, zp],
+            device_id={"dp": line, "expert": cn},
+            device_id_type=MESH,
+        )
+
+    def own(zp, q):
+        return pltpu.make_async_copy(
+            p_ref.at[zp, 2 * q + core], mine.at[zp, q], local.at[q, zp]
+        )
+
+    def plane(kind, zp, source, target, to):
+        return pltpu.make_async_remote_copy(
+            src_ref=source,
+            dst_ref=target,
+            send_sem=send.at[kind, zp],
+            recv_sem=recv.at[kind, zp],
+            device_id={"dp": line, "expert": to},
+            device_id_type=MESH,
+        )
+
+    def early(zp):
+        return (
+            plane(4, zp, mine.at[zp, apart, first], xa.at[zp, 1], xn),
+            plane(5, zp, mine.at[zp, apart, second], ya.at[zp, 1], yn),
+            plane(6, zp, mine.at[zp, beside, first], xa.at[zp, 0], xn),
+            plane(7, zp, mine.at[zp, over, second], ya.at[zp, 0], yn),
+        )
+
+    def late(zp):
+        return (
+            plane(8, zp, mine.at[zp, over, first], yb.at[zp], yn),
+            plane(9, zp, mine.at[zp, beside, second], xb.at[zp], xn),
+        )
+
+    def upwards(zp, to):
+        return pltpu.make_async_remote_copy(
+            src_ref=mine.at[zp, here],
+            dst_ref=below.at[zp],
+            send_sem=send.at[10, zp],
+            recv_sem=recv.at[10, zp],
+            device_id={"dp": to, "expert": spot},
+            device_id_type=MESH,
+        )
+
+    def downwards(zp, to):
+        return pltpu.make_async_remote_copy(
+            src_ref=mine.at[zp, here],
+            dst_ref=above.at[zp],
+            send_sem=send.at[11, zp],
+            recv_sem=recv.at[11, zp],
+            device_id={"dp": to, "expert": spot},
+            device_id_type=MESH,
+        )
+
+    def add(zp, q, start, count, other):
+        step = 16
+
+        def body(i, carry):
+            r = pl.multiple_of(i * step, step)
+            target = mine.at[zp, q, pl.ds(start + r, step)]
+            total = target[...].astype(jnp.float32) + other[pl.ds(r, step)].astype(jnp.float32)
+            target[...] = total.astype(jnp.bfloat16)
+            return carry
+
+        lax.fori_loop(0, count // step, body, 0)
+
+    if nz > 1:
+        low = line < nz // 2
+        order = [jnp.where(low, nz - 1 - k, k) for k in range(nz)]
+    else:
+        order = [0]
+    sequence = (apart, beside, over, here)
+    for zp in order:
+        for q in sequence:
+            own(zp, q).start()
+    greet(nz, line, (xn, yn, cn))
+    for zp in order:
+        for q in sequence:
+            sibling(zp, q).start()
+
+    def stage_one(zp):
+        for q in sequence:
+            own(zp, q).wait()
+            sibling(zp, q).wait_recv()
+            add(zp, q, 0, rows, sib.at[zp, q])
+            if q is apart:
+                early(zp)[0].start()
+                early(zp)[1].start()
+            elif q is beside:
+                early(zp)[2].start()
+            elif q is over:
+                early(zp)[3].start()
+
+    def stage_two(zp):
+        copies = early(zp)
+        copies[0].wait_recv()
+        add(zp, over, 0, half, xa.at[zp, 1])
+        late(zp)[0].start()
+        copies[1].wait_recv()
+        copies[2].wait_recv()
+        add(zp, here, 0, half, xa.at[zp, 0])
+        copies[3].wait_recv()
+        add(zp, here, half, half, ya.at[zp, 0])
+        add(zp, beside, half, half, ya.at[zp, 1])
+        late(zp)[1].start()
+
+    def stage_three(zp):
+        copies = late(zp)
+        copies[0].wait_recv()
+        add(zp, here, 0, half, yb.at[zp])
+        copies[1].wait_recv()
+        add(zp, here, half, half, xb.at[zp])
+        if nz > 1:
+
+            @pl.when((zp >= line) & (line > 0))
+            def _():
+                upwards(zp, line).wait_recv()
+                add(zp, here, 0, rows, below.at[zp])
+
+            @pl.when((zp <= line) & (line < nz - 1))
+            def _():
+                downwards(zp, line).wait_recv()
+                add(zp, here, 0, rows, above.at[zp])
+
+            @pl.when(zp > line)
+            def _():
+                upwards(zp, line + 1).start()
+
+            @pl.when(zp < line)
+            def _():
+                downwards(zp, line - 1).start()
+
+    for k in range(nz + 2):
+        if k < nz:
+            stage_one(order[k])
+        if 0 <= k - 1 < nz:
+            stage_two(order[k - 1])
+        if 0 <= k - 2 < nz:
+            stage_three(order[k - 2])
+    out_ref[...] = mine[zi, here]
+    for zp in order:
+        for q in sequence:
+            sibling(zp, q).wait_send()
+        for copy in early(zp) + late(zp):
+            copy.wait_send()
+        if nz > 1:
+
+            @pl.when(zp > line)
+            def _():
+                upwards(zp, line + 1).wait_send()
+
+            @pl.when(zp < line)
+            def _():
+                downwards(zp, line - 1).wait_send()
+
+
+def scatter_sum(p, number):
+    nz, _, rows, width = p.shape
+    half = rows // 2
+    kind = p.dtype
+    return pl.pallas_call(
+        functools.partial(scatter_kernel, nz),
+        out_shape=jax.ShapeDtypeStruct((rows, width), kind),
+        in_specs=[pl.BlockSpec(memory_space=pl.ANY)],
+        out_specs=pl.BlockSpec(memory_space=pltpu.VMEM),
+        scratch_shapes=[
+            pltpu.VMEM((nz, 4, rows, width), kind),
+            pltpu.VMEM((nz, 4, rows, width), kind),
+            pltpu.VMEM((nz, 2, half, width), kind),
+            pltpu.VMEM((nz, 2, half, width), kind),
+            pltpu.VMEM((nz, half, width), kind),
+            pltpu.VMEM((nz, half, width), kind),
+            pltpu.VMEM((nz, rows, width), kind),
+            pltpu.VMEM((nz, rows, width), kind),
+            pltpu.SemaphoreType.DMA((4, nz)),
+            pltpu.SemaphoreType.DMA((12, nz)),
+            pltpu.SemaphoreType.DMA((12, nz)),
+        ],
+        compiler_params=pltpu.CompilerParams(
+            collective_id=number, has_side_effects=True, vmem_limit_bytes=48 * 2**20
+        ),
+    )(p)
+
+
+def expert_kernel(capacity, x_ref, slot_ref, share_ref, gate_ref, up_ref, down_ref, out_ref, rows):
+    blocks, tokens, width = x_ref.shape[1:]
+    spots = lax.broadcasted_iota(jnp.int32, (capacity, tokens), 0)
+
+    def select(b):
+        return jnp.where(spots == slot_ref[0, b : b + 1, :], 1.0, 0.0).astype(jnp.bfloat16)
+
+    for b in range(blocks):
+        rows[b * capacity : (b + 1) * capacity, :] = jnp.dot(
+            select(b), x_ref[0, b], preferred_element_type=jnp.float32
+        ).astype(jnp.bfloat16)
+    flat = rows[...]
+    gated = jnp.dot(flat, gate_ref[0], preferred_element_type=jnp.float32)
+    lifted = jnp.dot(flat, up_ref[0], preferred_element_type=jnp.float32)
+    hidden = (gated / (1.0 + jnp.exp(-gated)) * lifted).astype(jnp.bfloat16)
+    rows[...] = jnp.dot(hidden, down_ref[0], preferred_element_type=jnp.float32).astype(
+        jnp.bfloat16
+    )
+    for b in range(blocks):
+        spread = lax.dot_general(
+            select(b),
+            rows[b * capacity : (b + 1) * capacity, :],
+            (((0,), (0,)), ((), ())),
+            preferred_element_type=jnp.float32,
+        )
+        out_ref[0, b] = (spread * share_ref[0, b]).astype(jnp.bfloat16)
+
+
+def expert_partials(x, slots, shares, gate_weight, up_weight, down_weight, capacity):
+    nz, blocks, tokens, width = x.shape
+    hidden_units = gate_weight.shape[2]
+    once = pl.Buffered(1)
+    return pl.pallas_call(
+        functools.partial(expert_kernel, capacity),
+        grid=(nz,),
+        out_shape=jax.ShapeDtypeStruct(x.shape, jnp.bfloat16),
+        in_specs=[
+            pl.BlockSpec((1, blocks, tokens, width), lambda i: (i, 0, 0, 0)),
+            pl.BlockSpec((1, blocks, tokens), lambda i: (i, 0, 0)),
+            pl.BlockSpec((1, blocks, tokens, 1), lambda i: (i, 0, 0, 0)),
+            pl.BlockSpec((1, width, hidden_units), lambda i: (0, 0, 0), pipeline_mode=once),
+            pl.BlockSpec((1, width, hidden_units), lambda i: (0, 0, 0), pipeline_mode=once),
+            pl.BlockSpec((1, hidden_units, width), lambda i: (0, 0, 0), pipeline_mode=once),
+        ],
+        out_specs=pl.BlockSpec((1, blocks, tokens, width), lambda i: (i, 0, 0, 0)),
+        scratch_shapes=[pltpu.VMEM((blocks * capacity, width), jnp.bfloat16)],
+        compiler_params=pltpu.CompilerParams(vmem_limit_bytes=52 * 2**20),
+        cost_estimate=pl.CostEstimate(
+            flops=6 * nz * blocks * capacity * width * hidden_units,
+            bytes_accessed=4 * nz * blocks * tokens * width,
+            transcendentals=0,
+        ),
+    )(x, slots, shares, gate_weight, up_weight, down_weight)
+
+
+def experts_by_plane(expert_input, expert_ids, expert_mix, gate_weight, up_weight, down_weight):
+    tok_rows = expert_input.shape[0]
+    nz, spots = lax.axis_size("dp"), lax.axis_size("expert")
+    devices = nz * spots
+    capacity = max(2, tok_rows * TOP * 3 // (2 * devices))
+    ids = lax.all_gather(expert_ids, ("dp", "expert"), axis=0, tiled=True)
+    mix = lax.all_gather(expert_mix, ("dp", "expert"), axis=0, tiled=True)
+    me = lax.axis_index("dp") * spots + lax.axis_index("expert")
+    named = ids == me
+    hit = jnp.any(named, axis=1).reshape(devices, tok_rows)
+    shares = jnp.sum(jnp.where(named, mix, 0.0), axis=1).reshape(nz, spots, tok_rows, 1)
+    before = jnp.triu(jnp.ones((tok_rows, tok_rows), jnp.bfloat16), 1)
+    slots = jnp.dot(hit.astype(jnp.bfloat16), before, preferred_element_type=jnp.float32)
+    slots = jnp.where(hit, slots.astype(jnp.int32), -1).reshape(nz, spots, tok_rows)
+    gathered = gather_rows(expert_input, nz, 2)
+    partials = expert_partials(
+        gathered, slots, shares, gate_weight, up_weight, down_weight, capacity
+    )
+    return scatter_sum(partials, 3)
 
 
 def per_device(
@@ -57,7 +545,11 @@
     longest = prompt_keys.shape[1]
     groups_here = prompt_keys.shape[0]
     normed = rms_scale(residual_in, attention_gain)
-    piece = lax.all_gather(normed, "expert", axis=0, tiled=True)
+    planar = lax.axis_size("expert") == 8 and gate_weight.shape[2] == FF
+    if planar:
+        piece = gather_rows(normed, 1, 0).reshape(-1, width)
+    else:
+        piece = lax.all_gather(normed, "expert", axis=0, tiled=True)
     query_part = jnp.dot(piece, query_weight, preferred_element_type=jnp.float32).astype(
         jnp.bfloat16
     )
@@ -122,15 +614,23 @@
     attended = lax.fori_loop(0, groups_here, group_step, jnp.zeros(layout, jnp.bfloat16))
     flat_attended = attended.reshape(requests * SB, local_width)
     piece = flat_attended
-    attention_update = lax.psum_scatter(
-        jnp.dot(piece, output_weight, preferred_element_type=jnp.float32).astype(jnp.bfloat16),
-        "expert",
-        scatter_dimension=0,
-        tiled=True,
-    )
+    update_part = jnp.dot(piece, output_weight, preferred_element_type=jnp.float32).astype(
+        jnp.bfloat16
+    )
+    if planar:
+        attention_update = scatter_sum(update_part.reshape(1, 8, tok_rows, width), 1)
+    else:
+        attention_update = lax.psum_scatter(
+            update_part, "expert", scatter_dimension=0, tiled=True
+        )
     expert_input = rms_scale(
         residual_in.astype(jnp.float32) + attention_update.astype(jnp.float32), expert_gain
     )
+    if planar:
+        expert_update = experts_by_plane(
+            expert_input, expert_ids, expert_mix, gate_weight, up_weight, down_weight
+        )
+        return (attention_update, expert_update)
     data_groups = lax.axis_size("dp")
     expert_groups = lax.axis_size("expert")
     devices = data_groups * expert_groups

time: 556 us -> 407 us (0.73)
  Pallas kernels: 0 us -> 251 us
  waiting for transfers between devices: 216 us -> 0 us
  blocking collectives: 143 us -> 81 us
  matrix products: 70.6 us -> 22.8 us
  local copies, waits for them, and re-layouts: 64.9 us -> 26.9 us
  other arithmetic: 39.4 us -> 20.8 us
  between operations: 14.2 us -> 0.82 us
    pallas_call x0 -> x5, Pallas kernels: none -> 251 us  [the longest x2 118 us: scatter_sum(): pl.pallas_call(functools.partial(scatter_kernel, nz), out_shape=jax.Shape...]
    all_to_all x1 -> x0, blocking collectives: 143 us -> none  [per_device(): lax.all_to_all(outgoing, ('dp', 'expert'), split_axis=0, concat_axis=0, t...]
    all_to_all x1 -> x0, waiting for transfers between devices: 140 us -> none  [per_device(): lax.all_to_all(expert_block(lax.all_to_all(outgoing, ('dp', 'expert'), sp...]
    all_gather x0 -> x2, blocking collectives: none -> 81 us  [the longest x1 43.8 us: experts_by_plane(): ids = lax.all_gather(expert_ids, ('dp', 'expert'), axis=0, tiled=True)]
    all_gather x1 -> x0, waiting for transfers between devices: 38.8 us -> none  [per_device(): piece = lax.all_gather(normed, 'expert', axis=0, tiled=True)]
    reduce_scatter x1 -> x0, waiting for transfers between devices: 37.3 us -> none  [per_device(): lax.psum_scatter(jnp.dot(piece, output_weight, preferred_element_type=jnp...]
    gather x2 -> x0, local copies, waits for them, and re-layouts: 32.6 us -> none  [the longest x1 25.5 us: per_device(): returned.reshape(experts, hidden_split, capacity, width)[chosen, :, slots]]
    dot_general x2 -> x1, matrix products: 29.1 us -> 0.13 us  [experts_by_plane(): jnp.dot(hit.astype(jnp.bfloat16), before, preferred_element_type=jnp.floa...]
  transfers between devices with their start and end apart: 3 -> 0, of which waited for: 3 -> 0; matrix products, arithmetic and copies ran while one was open for 3% -> 0% of each run, Pallas kernels for 0% -> 0%
where the time goes in v1:
time: 407 us
  Pallas kernels  251 us (62%)
  blocking collectives  81 us (20%)
  local copies, waits for them, and re-layouts  26.9 us (7%)
  matrix products  22.8 us (6%)
  other arithmetic  20.8 us (5%)
    pallas_call x2, Pallas kernels, scatter_sum(): pl.pallas_call(functools.partial(scatter_kernel, nz), out_shape=jax.Shape...  118 us
    pallas_call x2, Pallas kernels, gather_rows(): pl.pallas_call(functools.partial(gather_kernel, nz), out_shape=jax.ShapeD...  97.8 us
    all_gather x1, blocking collectives, experts_by_plane(): ids = lax.all_gather(expert_ids, ('dp', 'expert'), axis=0, tiled=True)  43.8 us
    all_gather x1, blocking collectives, experts_by_plane(): mix = lax.all_gather(expert_mix, ('dp', 'expert'), axis=0, tiled=True)  37.2 us
    pallas_call x1, Pallas kernels, expert_partials(): pl.pallas_call(functools.partial(expert_kernel, capacity), grid=(nz,), ou...  35.3 us

profile of v1, /device:TPU:0, one launch (start us, length us, event | category | flops | bytes accessed | tf_op | source)
XLA Modules:
  0.0 406.6 jit_solution(6106541986099142097)
XLA Ops:
  2.8 43.8 %all_gather.6 = s32[4096,8]{0,1:T(8,128)S(1)} all-gather(s32[128,8]{0,1:T(8,128)} %param.31), channel_id=1, replica_groups=mesh['dp'=4,'expert'=8] {'dp','expert'}, dimensions={0}, use_global_device_ids=true | all-gather | bytes 135168 | tf_op jit(solution)/shard_map/all_gather | solution.py:506
  46.6 37.2 %all_gather.7 = f32[4096,8]{0,1:T(8,128)S(1)} all-gather(f32[128,8]{0,1:T(8,128)} %param.32), channel_id=1, replica_groups=mesh['dp'=4,'expert'=8] {'dp','expert'}, dimensions={0}, use_global_device_ids=true | all-gather | bytes 135168 | tf_op jit(solution)/shard_map/all_gather | solution.py:507
  84.0 2.0 fusion.20.x_ref
  86.1 2.0 copy.63.share_ref
  88.0 24.5 %shard_map.176 = bf16[1,8,128,2048]{3,2,1,0:T(8,128)(2,1)} custom-call(bf16[128,2048]{1,0:T(8,128)(2,1)} %fusion.20.x_ref), custom_call_target="tpu_custom_call" | custom-call | tf_op jit(solution)/shard_map/pallas_call | solution.py:227
  112.6 3.4 convolution_convert_fusion.1
  116.9 3.8 convolution_convert_fusion.2
  120.7 3.7 convolution_convert_fusion.3
  125.6 50.0 %while.14 = (s32[]{:T(128)}, bf16[32,32,2,128]{3,2,1,0:T(2,128)(2,1)S(1)}, s32[32]{0:T(128)S(1)}, bf16[3,2048,256]{2,1,0:T(8,128)(2,1)}, s32[3]{0:T(128)S(1)}, /...) while((s32[]{:T(128)}, ...), condition=%wide.region_7.8_spmd.clone, body=%wide.region_1.7_spmd.clone.sunk | while | flops 1110081664 | bytes 66003656 | solution.py:614
  129.3 2.2 constant_dynamic-slice_fusion.10
  131.5 1.7 constant_dynamic-slice_fusion.8
  137.5 1.8 convolution_bitcast_fusion.3
  139.4 1.9 convert_reduce_fusion.5
  145.9 2.2 constant_dynamic-slice_fusion.10
  148.1 1.7 constant_dynamic-slice_fusion.8
  154.1 1.8 convolution_bitcast_fusion.3
  156.0 1.9 convert_reduce_fusion.5
  162.5 2.2 constant_dynamic-slice_fusion.10
  170.7 1.8 convolution_bitcast_fusion.3
  172.6 1.9 convert_reduce_fusion.5
  176.9 23.9 %shard_map.177 = bf16[128,2048]{1,0:T(8,128)(2,1)S(1)} custom-call(bf16[1,8,128,2048]{3,2,1,0:T(8,128)(2,1)S(1)} %bitcast.87), custom_call_target="tpu_custom_call" | custom-call | tf_op jit(solution)/shard_map/pallas_call | solution.py:422
  202.1 73.3 %shard_map.178.x_ref = bf16[4,8,128,2048]{3,2,1,0:T(8,128)(2,1)} custom-call(bf16[128,2048]{1,0:T(8,128)(2,1)} %multiply_convert_fusion.x_ref), custom_call_target="tpu_custom_call" | custom-call | tf_op jit(solution)/shard_map/pallas_call | solution.py:227
  275.4 35.3 %shard_map.179.p_ref = bf16[4,8,128,2048]{3,2,1,0:T(8,128)(2,1)} custom-call(bf16[4,8,128,2048]{3,2,1,0:T(8,128)(2,1)} %shard_map.178.x_ref, s32[4,8,128]{2,1,0:T(8,128)S(1)} %fusion.17.slot_ref, f32[4,8,128,1]{3,2,1,0:T(8,128)} %copy.63.share_ref, bf16[1,2048,1024]{2,1,0:T(8,128)(2,1)} %gate_ref.1, bf16[1,2048,1024]{2,1,0:T(8,128)(2,1)} %up_ref.1, ...), custom_call_target="tpu_custom_call" | custom-call | flops 19327352832 | bytes 33554432 | tf_op jit(solution)/shard_map/pallas_call | solution.py:478
  310.6 94.4 %shard_map.180 = bf16[128,2048]{1,0:T(8,128)(2,1)S(1)} custom-call(bf16[4,8,128,2048]{3,2,1,0:T(8,128)(2,1)} %shard_map.179.p_ref), custom_call_target="tpu_custom_call" | custom-call | tf_op jit(solution)/shard_map/pallas_call | solution.py:422
  (135 shorter events, 34.3 us)
Async XLA Ops:
  0.6 175.0 %copy-start = (bf16[256,2048]{1,0:T(8,128)(2,1)S(1)}, bf16[256,2048]{1,0:T(8,128)(2,1)}, u32[]{:S(2)}) copy-start(bf16[256,2048]{1,0:T(8,128)(2,1)} %param.24) | copy-start | bytes 3145732
  0.6 111.9 %copy-start.13 = (bf16[2048,256]{1,0:T(8,128)(2,1)S(1)}, bf16[2048,256]{1,0:T(8,128)(2,1)}, u32[]{:S(2)}) copy-start(bf16[2048,256]{1,0:T(8,128)(2,1)} %param.23) | copy-start | bytes 3145732
  116.9 8.6 %copy-start.11 = (s32[1,32]{1,0:T(1,128)S(1)}, s32[1,32]{1,0:T(1,128)}, u32[]{:S(2)}) copy-start(s32[1,32]{1,0:T(1,128)} %param.27) | copy-start | bytes 388
  116.9 8.7 %copy-start.14 = (s32[3]{0:T(128)S(1)}, s32[3]{0:T(128)}, u32[]{:S(2)}) copy-start(s32[3]{0:T(128)} %param.28) | copy-start | bytes 40
  125.8 3.2 copy-start.9
  125.8 5.7 %copy-start.1 = (f32[32,2,32,32]{3,2,1,0:T(8,128)}, f32[32,2,32,32]{3,2,1,0:T(8,128)S(1)}, u32[]{:S(2)}) copy-start(f32[32,2,32,32]{3,2,1,0:T(8,128)S(1)} %get-tuple-element.354) | copy-start | bytes 786436 | tf_op jit(solution)/shard_map/while
  125.8 5.7 %copy-start.4 = (bf16[32,32,2,128]{3,2,1,0:T(2,128)(2,1)}, bf16[32,32,2,128]{3,2,1,0:T(2,128)(2,1)S(1)}, u32[]{:S(2)}) copy-start(bf16[32,32,2,128]{3,2,1,0:T(2,128)(2,1)S(1)} %get-tuple-element.335) | copy-start | bytes 1572868 | tf_op jit(solution)/shard_map/while
  139.3 2.4 copy-start.7
  139.4 2.4 copy-start.8
  139.4 2.7 copy-start.5
  139.4 3.0 copy-start.10
  142.4 3.2 copy-start.9
  142.4 5.7 %copy-start.1 = (f32[32,2,32,32]{3,2,1,0:T(8,128)}, f32[32,2,32,32]{3,2,1,0:T(8,128)S(1)}, u32[]{:S(2)}) copy-start(f32[32,2,32,32]{3,2,1,0:T(8,128)S(1)} %get-tuple-element.354) | copy-start | bytes 786436 | tf_op jit(solution)/shard_map/while
  142.4 5.7 %copy-start.4 = (bf16[32,32,2,128]{3,2,1,0:T(2,128)(2,1)}, bf16[32,32,2,128]{3,2,1,0:T(2,128)(2,1)S(1)}, u32[]{:S(2)}) copy-start(bf16[32,32,2,128]{3,2,1,0:T(2,128)(2,1)S(1)} %get-tuple-element.335) | copy-start | bytes 1572868 | tf_op jit(solution)/shard_map/while
  155.9 2.4 copy-start.7
  156.0 2.7 copy-start.5
  156.0 3.0 copy-start.10
  159.0 3.2 copy-start.9
  159.0 5.7 %copy-start.1 = (f32[32,2,32,32]{3,2,1,0:T(8,128)}, f32[32,2,32,32]{3,2,1,0:T(8,128)S(1)}, u32[]{:S(2)}) copy-start(f32[32,2,32,32]{3,2,1,0:T(8,128)S(1)} %get-tuple-element.354) | copy-start | bytes 786436 | tf_op jit(solution)/shard_map/while
  159.0 5.7 %copy-start.4 = (bf16[32,32,2,128]{3,2,1,0:T(2,128)(2,1)}, bf16[32,32,2,128]{3,2,1,0:T(2,128)(2,1)S(1)}, u32[]{:S(2)}) copy-start(bf16[32,32,2,128]{3,2,1,0:T(2,128)(2,1)S(1)} %get-tuple-element.335) | copy-start | bytes 1572868 | tf_op jit(solution)/shard_map/while
  172.6 2.7 copy-start.5
  172.6 3.0 copy-start.10
  175.6 25.2 %copy-start.6 = (bf16[128,2048]{1,0:T(8,128)(2,1)S(1)}, bf16[128,2048]{1,0:T(8,128)(2,1)}, u32[]{:S(2)}) copy-start(bf16[128,2048]{1,0:T(8,128)(2,1)} %param.19) | copy-start | bytes 1572868
  175.6 25.4 %copy-start.12 = (f32[2048]{0:T(1024)S(1)}, f32[2048]{0:T(1024)}, u32[]{:S(2)}) copy-start(f32[2048]{0:T(1024)} %param.30) | copy-start | bytes 24580
  (9 other events, 19.8 us)

commit v2 on v1

--- a/solution.py
+++ b/solution.py
@@ -443,16 +443,32 @@
     )(p)
 
 
-def expert_kernel(capacity, x_ref, slot_ref, share_ref, gate_ref, up_ref, down_ref, out_ref, rows):
-    blocks, tokens, width = x_ref.shape[1:]
-    spots = lax.broadcasted_iota(jnp.int32, (capacity, tokens), 0)
-
-    def select(b):
-        return jnp.where(spots == slot_ref[0, b : b + 1, :], 1.0, 0.0).astype(jnp.bfloat16)
-
+def expert_kernel(capacity, x_ref, gate_ref, up_ref, down_ref, out_ref, rows):
+    blocks, tokens = x_ref.shape[1:3]
+    width = out_ref.shape[3]
+    me = lax.axis_index("dp") * blocks + lax.axis_index("expert")
+    spots = lax.broadcasted_iota(jnp.int32, (tokens, capacity), 1).astype(jnp.float32)
+    earlier = lax.broadcasted_iota(jnp.int32, (tokens, tokens), 1)
+    earlier = earlier < lax.broadcasted_iota(jnp.int32, (tokens, tokens), 0)
+    earlier = jnp.where(earlier, 1.0, 0.0).astype(jnp.bfloat16)
+    mine = me.astype(jnp.float32)
+    places, shares = [], []
     for b in range(blocks):
-        rows[b * capacity : (b + 1) * capacity, :] = jnp.dot(
-            select(b), x_ref[0, b], preferred_element_type=jnp.float32
+        extra = x_ref[0, b, :, width:].astype(jnp.float32)
+        named = extra[:, :TOP] == mine
+        mix = extra[:, TOP : 2 * TOP] + extra[:, 2 * TOP : 3 * TOP]
+        mix = mix + extra[:, 3 * TOP : 4 * TOP]
+        shares.append(jnp.sum(jnp.where(named, mix, 0.0), axis=1, keepdims=True))
+        hit = jnp.sum(jnp.where(named, 1.0, 0.0), axis=1, keepdims=True)
+        hit = jnp.broadcast_to(hit, (tokens, capacity))
+        slots = jnp.dot(earlier, hit.astype(jnp.bfloat16), preferred_element_type=jnp.float32)
+        place = jnp.where((hit > 0.5) & (slots == spots), 1.0, 0.0).astype(jnp.bfloat16)
+        places.append(place)
+        rows[b * capacity : (b + 1) * capacity, :] = lax.dot_general(
+            place,
+            x_ref[0, b, :, :width],
+            (((0,), (0,)), ((), ())),
+            preferred_element_type=jnp.float32,
         ).astype(jnp.bfloat16)
     flat = rows[...]
     gated = jnp.dot(flat, gate_ref[0], preferred_element_type=jnp.float32)
@@ -462,27 +478,25 @@
         jnp.bfloat16
     )
     for b in range(blocks):
-        spread = lax.dot_general(
-            select(b),
+        spread = jnp.dot(
+            places[b],
             rows[b * capacity : (b + 1) * capacity, :],
-            (((0,), (0,)), ((), ())),
             preferred_element_type=jnp.float32,
         )
-        out_ref[0, b] = (spread * share_ref[0, b]).astype(jnp.bfloat16)
-
-
-def expert_partials(x, slots, shares, gate_weight, up_weight, down_weight, capacity):
-    nz, blocks, tokens, width = x.shape
+        out_ref[0, b] = (spread * shares[b]).astype(jnp.bfloat16)
+
+
+def expert_partials(x, gate_weight, up_weight, down_weight, capacity):
+    nz, blocks, tokens, wide = x.shape
+    width = gate_weight.shape[1]
     hidden_units = gate_weight.shape[2]
     once = pl.Buffered(1)
     return pl.pallas_call(
         functools.partial(expert_kernel, capacity),
         grid=(nz,),
-        out_shape=jax.ShapeDtypeStruct(x.shape, jnp.bfloat16),
+        out_shape=jax.ShapeDtypeStruct((nz, blocks, tokens, width), jnp.bfloat16),
         in_specs=[
-            pl.BlockSpec((1, blocks, tokens, width), lambda i: (i, 0, 0, 0)),
-            pl.BlockSpec((1, blocks, tokens), lambda i: (i, 0, 0)),
-            pl.BlockSpec((1, blocks, tokens, 1), lambda i: (i, 0, 0, 0)),
+            pl.BlockSpec((1, blocks, tokens, wide), lambda i: (i, 0, 0, 0)),
             pl.BlockSpec((1, width, hidden_units), lambda i: (0, 0, 0), pipeline_mode=once),
             pl.BlockSpec((1, width, hidden_units), lambda i: (0, 0, 0), pipeline_mode=once),
             pl.BlockSpec((1, hidden_units, width), lambda i: (0, 0, 0), pipeline_mode=once),
@@ -495,7 +509,7 @@
             bytes_accessed=4 * nz * blocks * tokens * width,
             transcendentals=0,
         ),
-    )(x, slots, shares, gate_weight, up_weight, down_weight)
+    )(x, gate_weight, up_weight, down_weight)
 
 
 def experts_by_plane(expert_input, expert_ids, expert_mix, gate_weight, up_weight, down_weight):
@@ -503,19 +517,15 @@
     nz, spots = lax.axis_size("dp"), lax.axis_size("expert")
     devices = nz * spots
     capacity = max(2, tok_rows * TOP * 3 // (2 * devices))
-    ids = lax.all_gather(expert_ids, ("dp", "expert"), axis=0, tiled=True)
-    mix = lax.all_gather(expert_mix, ("dp", "expert"), axis=0, tiled=True)
-    me = lax.axis_index("dp") * spots + lax.axis_index("expert")
-    named = ids == me
-    hit = jnp.any(named, axis=1).reshape(devices, tok_rows)
-    shares = jnp.sum(jnp.where(named, mix, 0.0), axis=1).reshape(nz, spots, tok_rows, 1)
-    before = jnp.triu(jnp.ones((tok_rows, tok_rows), jnp.bfloat16), 1)
-    slots = jnp.dot(hit.astype(jnp.bfloat16), before, preferred_element_type=jnp.float32)
-    slots = jnp.where(hit, slots.astype(jnp.int32), -1).reshape(nz, spots, tok_rows)
-    gathered = gather_rows(expert_input, nz, 2)
-    partials = expert_partials(
-        gathered, slots, shares, gate_weight, up_weight, down_weight, capacity
-    )
+    high = lax.reduce_precision(expert_mix, 8, 7)
+    middle = lax.reduce_precision(expert_mix - high, 8, 7)
+    low = expert_mix - high - middle
+    routes = jnp.concatenate(
+        [part.astype(jnp.bfloat16) for part in (expert_ids, high, middle, low)], axis=1
+    )
+    routes = jnp.pad(routes, ((0, 0), (0, 128 - routes.shape[1])))
+    gathered = gather_rows(jnp.concatenate([expert_input, routes], axis=1), nz, 2)
+    partials = expert_partials(gathered, gate_weight, up_weight, down_weight, capacity)
     return scatter_sum(partials, 3)
 
 

time: 407 us -> 336 us (0.83)
  blocking collectives: 81 us -> 0 us
  Pallas kernels: 251 us -> 264 us
    all_gather x2 -> x0, blocking collectives: 81 us -> none  [the longest x1 43.8 us: experts_by_plane(): ids = lax.all_gather(expert_ids, ('dp', 'expert'), axis=0, tiled=True)]
    pallas_call x2, Pallas kernels: 97.8 us -> 104 us  [gather_rows(): pl.pallas_call(functools.partial(gather_kernel, nz), out_shape=jax.ShapeD...]
    pallas_call x1, Pallas kernels: 35.3 us -> 41.5 us  [expert_partials(): pl.pallas_call(functools.partial(expert_kernel, capacity), grid=(nz,), ou...]
where the time goes in v2:
time: 336 us; the launch traced here: 335 us
  Pallas kernels  264 us (79%)
  local copies, waits for them, and re-layouts  25.7 us (8%)
  other arithmetic  21.9 us (7%)
  matrix products  20.2 us (6%)
    pallas_call x2, Pallas kernels, scatter_sum(): pl.pallas_call(functools.partial(scatter_kernel, nz), out_shape=jax.Shape...  118 us
    pallas_call x2, Pallas kernels, gather_rows(): pl.pallas_call(functools.partial(gather_kernel, nz), out_shape=jax.ShapeD...  104 us
    pallas_call x1, Pallas kernels, expert_partials(): pl.pallas_call(functools.partial(expert_kernel, capacity), grid=(nz,), ou...  41.5 us
    dynamic_slice x6, local copies, waits for them, and re-layouts, group_step(): lax.dynamic_index_in_dim(prompt_keys, group, 0, keepdims=False)  6.94 us

profile of v2, /device:TPU:0, one launch (start us, length us, event | category | flops | bytes accessed | tf_op | source)
XLA Modules:
  0.0 335.2 jit_solution(7580569063460736743)
XLA Ops:
  4.3 2.0 fusion.19.x_ref
  6.3 25.7 %shard_map.176 = bf16[1,8,128,2048]{3,2,1,0:T(8,128)(2,1)} custom-call(bf16[128,2048]{1,0:T(8,128)(2,1)} %fusion.19.x_ref), custom_call_target="tpu_custom_call" | custom-call | tf_op jit(solution)/shard_map/pallas_call | solution.py:227
  32.0 3.4 %convolution_convert_fusion.1 = bf16[1024,256]{1,0:T(8,128)(2,1)S(1)} fusion(bf16[1024,2048]{1,0:T(8,128)(2,1)} %bitcast.89, bf16[2048,256]{1,0:T(8,128)(2,1)S(1)} %copy-done.14), kind=kOutput, calls=%fused_computation.39 | convolution fusion | flops 1074003968 | bytes 5767168 | tf_op jit(solution)/shard_map/dot_general | solution.py:567
  36.4 3.9 %convolution_convert_fusion.2 = bf16[1024,256]{1,0:T(8,128)(2,1)S(1)} fusion(bf16[1024,2048]{1,0:T(8,128)(2,1)} %bitcast.90, bf16[2048,256]{1,0:T(8,128)(2,1)} %param.22), kind=kOutput, calls=%fused_computation.40 | convolution fusion | flops 1074003968 | bytes 5767168 | tf_op jit(solution)/shard_map/dot_general | solution.py:566
  42.7 50.1 %while.14 = (s32[]{:T(128)}, bf16[32,32,2,128]{3,2,1,0:T(2,128)(2,1)S(1)}, s32[32]{0:T(128)S(1)}, bf16[3,2048,256]{2,1,0:T(8,128)(2,1)}, s32[3]{0:T(128)S(1)}, /...) while((s32[]{:T(128)}, ...), condition=%wide.region_7.8_spmd.clone, body=%wide.region_1.7_spmd.clone.sunk | while | flops 1110081664 | bytes 66003656 | solution.py:624
  46.2 2.2 constant_dynamic-slice_fusion.10
  48.4 1.7 constant_dynamic-slice_fusion.8
  50.1 1.4 copy.116
  54.7 1.8 convolution_bitcast_fusion.3
  56.5 1.9 convert_reduce_fusion.5
  62.8 2.2 constant_dynamic-slice_fusion.10
  65.1 1.7 constant_dynamic-slice_fusion.8
  66.7 1.4 copy.116
  71.3 1.8 convolution_bitcast_fusion.3
  73.1 1.9 convert_reduce_fusion.5
  79.5 2.2 constant_dynamic-slice_fusion.10
  81.7 1.7 constant_dynamic-slice_fusion.8
  83.4 1.4 copy.116
  87.9 1.8 convolution_bitcast_fusion.3
  89.8 1.9 convert_reduce_fusion.5
  94.1 23.9 %shard_map.177 = bf16[128,2048]{1,0:T(8,128)(2,1)S(1)} custom-call(bf16[1,8,128,2048]{3,2,1,0:T(8,128)(2,1)S(1)} %bitcast.81), custom_call_target="tpu_custom_call" | custom-call | tf_op jit(solution)/shard_map/pallas_call | solution.py:422
  119.4 78.5 %shard_map.178.x_ref = bf16[4,8,128,2176]{3,2,1,0:T(8,128)(2,1)} custom-call(bf16[128,2176]{1,0:T(8,128)(2,1)} %fusion.20.x_ref), custom_call_target="tpu_custom_call" | custom-call | tf_op jit(solution)/shard_map/pallas_call | solution.py:227
  197.9 41.5 %shard_map.179.p_ref = bf16[4,8,128,2048]{3,2,1,0:T(8,128)(2,1)} custom-call(bf16[4,8,128,2176]{3,2,1,0:T(8,128)(2,1)} %shard_map.178.x_ref, bf16[1,2048,1024]{2,1,0:T(8,128)(2,1)} %gate_ref.1, bf16[1,2048,1024]{2,1,0:T(8,128)(2,1)} %up_ref.1, bf16[1,1024,2048]{2,1,0:T(8,128)(2,1)} %down_ref.1), custom_call_target="tpu_custom_call" | custom-call | flops 19327352832 | bytes 33554432 | tf_op jit(solution)/shard_map/pallas_call | solution.py:494
  239.4 94.2 %shard_map.180 = bf16[128,2048]{1,0:T(8,128)(2,1)S(1)} custom-call(bf16[4,8,128,2048]{3,2,1,0:T(8,128)(2,1)} %shard_map.179.p_ref), custom_call_target="tpu_custom_call" | custom-call | tf_op jit(solution)/shard_map/pallas_call | solution.py:422
  (138 shorter events, 31.3 us)
Async XLA Ops:
  0.6 92.2 %copy-start = (bf16[256,2048]{1,0:T(8,128)(2,1)S(1)}, bf16[256,2048]{1,0:T(8,128)(2,1)}, u32[]{:S(2)}) copy-start(bf16[256,2048]{1,0:T(8,128)(2,1)} %param.24) | copy-start | bytes 3145732
  0.6 31.4 %copy-start.14 = (bf16[2048,256]{1,0:T(8,128)(2,1)S(1)}, bf16[2048,256]{1,0:T(8,128)(2,1)}, u32[]{:S(2)}) copy-start(bf16[2048,256]{1,0:T(8,128)(2,1)} %param.23) | copy-start | bytes 3145732
  35.4 4.8 %copy-start.15 = (bf16[2048,256]{1,0:T(8,128)(2,1)S(1)}, bf16[2048,256]{1,0:T(8,128)(2,1)}, u32[]{:S(2)}) copy-start(bf16[2048,256]{1,0:T(8,128)(2,1)} %param.21) | copy-start | bytes 3145732
  36.4 3.9 %copy-start.11 = (bf16[1,8,128,2048]{3,2,1,0:T(8,128)(2,1)S(1)}, bf16[1,8,128,2048]{3,2,1,0:T(8,128)(2,1)}, u32[]{:S(2)}) copy-start(bf16[1,8,128,2048]{3,2,1,0:T(8,128)(2,1)} %shard_map.176) | copy-start | bytes 12582916
  42.9 3.0 copy-start.9
  42.9 5.5 %copy-start.1 = (f32[32,2,32,32]{3,2,1,0:T(8,128)}, f32[32,2,32,32]{3,2,1,0:T(8,128)S(1)}, u32[]{:S(2)}) copy-start(f32[32,2,32,32]{3,2,1,0:T(8,128)S(1)} %get-tuple-element.355) | copy-start | bytes 786436 | tf_op jit(solution)/shard_map/while
  42.9 5.5 %copy-start.4 = (bf16[32,32,2,128]{3,2,1,0:T(2,128)(2,1)}, bf16[32,32,2,128]{3,2,1,0:T(2,128)(2,1)S(1)}, u32[]{:S(2)}) copy-start(bf16[32,32,2,128]{3,2,1,0:T(2,128)(2,1)S(1)} %get-tuple-element.336) | copy-start | bytes 1572868 | tf_op jit(solution)/shard_map/while
  56.5 2.4 copy-start.7
  56.5 2.4 copy-start.8
  56.5 2.7 copy-start.5
  59.5 3.0 copy-start.9
  59.5 5.5 %copy-start.1 = (f32[32,2,32,32]{3,2,1,0:T(8,128)}, f32[32,2,32,32]{3,2,1,0:T(8,128)S(1)}, u32[]{:S(2)}) copy-start(f32[32,2,32,32]{3,2,1,0:T(8,128)S(1)} %get-tuple-element.355) | copy-start | bytes 786436 | tf_op jit(solution)/shard_map/while
  59.6 5.5 %copy-start.4 = (bf16[32,32,2,128]{3,2,1,0:T(2,128)(2,1)}, bf16[32,32,2,128]{3,2,1,0:T(2,128)(2,1)S(1)}, u32[]{:S(2)}) copy-start(bf16[32,32,2,128]{3,2,1,0:T(2,128)(2,1)S(1)} %get-tuple-element.336) | copy-start | bytes 1572868 | tf_op jit(solution)/shard_map/while
  73.1 2.4 copy-start.7
  73.1 2.4 copy-start.8
  73.1 2.7 copy-start.5
  76.2 3.0 copy-start.9
  76.2 5.5 %copy-start.1 = (f32[32,2,32,32]{3,2,1,0:T(8,128)}, f32[32,2,32,32]{3,2,1,0:T(8,128)S(1)}, u32[]{:S(2)}) copy-start(f32[32,2,32,32]{3,2,1,0:T(8,128)S(1)} %get-tuple-element.355) | copy-start | bytes 786436 | tf_op jit(solution)/shard_map/while
  76.2 5.5 %copy-start.4 = (bf16[32,32,2,128]{3,2,1,0:T(2,128)(2,1)}, bf16[32,32,2,128]{3,2,1,0:T(2,128)(2,1)S(1)}, u32[]{:S(2)}) copy-start(bf16[32,32,2,128]{3,2,1,0:T(2,128)(2,1)S(1)} %get-tuple-element.336) | copy-start | bytes 1572868 | tf_op jit(solution)/shard_map/while
  89.7 2.4 copy-start.7
  89.8 2.4 copy-start.8
  89.8 2.7 copy-start.5
  94.1 23.9 %copy-start.6 = (bf16[128,2048]{1,0:T(8,128)(2,1)S(1)}, bf16[128,2048]{1,0:T(8,128)(2,1)}, u32[]{:S(2)}) copy-start(bf16[128,2048]{1,0:T(8,128)(2,1)} %param.19) | copy-start | bytes 1572868
  94.1 24.2 %copy-start.13 = (f32[2048]{0:T(1024)S(1)}, f32[2048]{0:T(1024)}, u32[]{:S(2)}) copy-start(f32[2048]{0:T(1024)} %param.30) | copy-start | bytes 24580
  (11 other events, 15.2 us)
